TPU v7x, 512 devices: a whole 4x8x8 slice. The times are simulated.
512 devices in a mesh: lon: 128 (over x_lo, y, z), lat: 4 (over x_hi, core).
Axes of the slice: x: 4 (x_hi: 2, x_lo: 2; x = x_hi * 2 + x_lo), y: 8, z: 8, core: 2. Of those that a mesh axis runs over, the one named last changes fastest.
Arguments:
- latent: bfloat16 [1, 48, 3072, 512], P(None, 'lat', 'lon'), may hold values from -6 to 6
- admit_mask: int32 [48, 3072], P('lat', 'lon'), may hold values 0 or 1
- fine_params: bfloat16 [1048576], P('lon')
- coarse_params: bfloat16 [6291456], P('lon')
Outputs:
- skip_tokens: bfloat16 [1, 48, 3072, 512], P(None, 'lat', 'lon')
- coarse_tokens: bfloat16 [1, 24, 1536, 1024], P(None, 'lat', 'lon')
All inputs are finite; a program needn't handle non-finite values. No bound on the sum of `admit_mask` on one device may be relied on, other than what follows from the above.
Results may differ from a plain program's by a relative error of at most 0.015.
Values may be sent and summed in bfloat16 or wider, within the bound.
No kernel may reach another device: no remote copies, remote signals or barrier semaphores. Data moves between devices by JAX's collectives and lax.ppermute only.
A program may use at most 128 MiB of HBM per device.

v0:
```python
import math

import jax
import jax.numpy as jnp
from jax import lax
from jax.sharding import PartitionSpec as P

FINE_HEADS = 8
COARSE_HEADS = 16
WIN_LAT = 6
WIN_LON = 12


epsilon = 1e-05


def with_halo(cells, sides, width, closed):
    for axis, dim in sides:
        count = lax.axis_size(axis)
        ends = count if closed else count - 1
        head = lax.slice_in_dim(cells, 0, width, axis=dim)
        tail = lax.slice_in_dim(cells, cells.shape[dim] - width, cells.shape[dim], axis=dim)
        cells = jnp.concatenate(
            [
                lax.ppermute(tail, axis, [(i, (i + 1) % count) for i in range(ends)]),
                cells,
                lax.ppermute(head, axis, [((i + 1) % count, i) for i in range(ends)]),
            ],
            axis=dim,
        )
    return cells


def layer_norm(values):
    values = values.astype(jnp.float32)
    centered = values - jnp.mean(values, axis=-1, keepdims=True)
    spread = jnp.mean(centered * centered, axis=-1, keepdims=True)
    return (centered * lax.rsqrt(spread + epsilon)).astype(jnp.bfloat16)


def project(values, matrix):
    return jnp.dot(values, matrix, preferred_element_type=jnp.float32).astype(jnp.bfloat16)


def attend(queries, key_values, admitted, head_count):
    levels, row_count, col_count, channels = queries.shape
    head_size = channels // head_count
    win_rows = row_count // WIN_LAT
    win_cols = col_count // WIN_LON
    window_len = levels * WIN_LAT * WIN_LON

    def windows(values, segments):
        arranged = values.reshape(
            levels, win_rows, WIN_LAT, win_cols, WIN_LON, segments, head_count, head_size
        )
        arranged = arranged.transpose(1, 3, 5, 6, 0, 2, 4, 7)
        return arranged.reshape(win_rows, win_cols, segments, head_count, window_len, head_size)

    query_win = windows(queries, 1)[:, :, 0]
    both = windows(key_values, 2)
    key_mask = admitted.reshape(win_rows, WIN_LAT, win_cols, WIN_LON).transpose(0, 2, 1, 3)
    key_mask = key_mask[:, :, None]
    key_mask = key_mask.reshape(win_rows, win_cols, window_len)
    diagonal = jnp.eye(window_len, dtype=bool)

    def one_row(items):
        row_queries, row_pairs, row_mask = items
        scores = jnp.einsum(
            "bhqd,bhkd->bhqk", row_queries, row_pairs[:, 0], preferred_element_type=jnp.float32
        ) / math.sqrt(head_size)
        allowed = (row_mask[:, None, None, :] > 0) | diagonal
        scores = jnp.where(allowed, scores, -jnp.inf)
        highest = jnp.max(scores, axis=-1, keepdims=True)
        raised = jnp.exp(scores - highest)
        attention = (raised / jnp.sum(raised, axis=-1, keepdims=True)).astype(jnp.bfloat16)
        return jnp.einsum(
            "bhqk,bhkd->bhqd", attention, row_pairs[:, 1], preferred_element_type=jnp.float32
        ).astype(jnp.bfloat16)

    blended = lax.map(one_row, (query_win, both, key_mask))
    blended = blended.reshape(win_rows, win_cols, head_count, levels, WIN_LAT, WIN_LON, head_size)
    blended = blended.transpose(3, 0, 4, 1, 5, 2, 6)
    return blended.reshape(levels, row_count, col_count, channels)


def local(latent, admit_mask, fine_params, coarse_params):
    channels = latent.shape[-1]
    levels = latent.shape[0]
    square = channels * channels
    lat_rows, lon_cols = admit_mask.shape
    rim_lat = WIN_LAT // 2
    rim_lon = WIN_LON // 2
    fine_flat = lax.all_gather(fine_params, "lon", axis=0, tiled=True)
    fine_inputs = fine_flat[: 3 * square].reshape(channels, 3 * channels)
    fine_output = fine_flat[3 * square :].reshape(channels, channels)
    normed = layer_norm(latent)
    queries = project(normed, fine_inputs[:, :channels])
    outgoing = project(normed, fine_inputs[:, channels:])
    admitted = admit_mask.astype(jnp.bfloat16)[None]
    outgoing, admitted = (
        with_halo(outgoing, (("lat", 1),), rim_lat, False),
        with_halo(admitted, (("lat", 1),), rim_lat, False),
    )
    outgoing, admitted = (
        with_halo(outgoing, (("lon", 2),), rim_lon, True),
        with_halo(admitted, (("lon", 2),), rim_lon, True),
    )
    padding = ((0, 0), (rim_lat, rim_lat), (rim_lon, rim_lon), (0, 0))
    blended = attend(
        jnp.pad(queries, padding), outgoing, admitted[0].astype(jnp.float32), FINE_HEADS
    )
    blended = blended[:, rim_lat : rim_lat + lat_rows, rim_lon : rim_lon + lon_cols]
    skip_tokens = (
        latent + jnp.dot(blended, fine_output, preferred_element_type=jnp.float32)
    ).astype(jnp.bfloat16)
    coarse_flat = lax.all_gather(coarse_params, "lon", axis=0, tiled=True)
    coarse_merge = coarse_flat[: 8 * square].reshape(4 * channels, 2 * channels)
    coarse_inputs = coarse_flat[8 * square : 20 * square].reshape(2 * channels, 6 * channels)
    coarse_output = coarse_flat[20 * square :].reshape(2 * channels, 2 * channels)
    stacked = skip_tokens.reshape(levels, lat_rows // 2, 2, lon_cols // 2, 2, channels).transpose(
        0, 1, 3, 4, 2, 5
    )
    stacked = stacked.reshape(levels, lat_rows // 2, lon_cols // 2, 4 * channels)
    merged = project(layer_norm(stacked), coarse_merge)
    coarse_normed = layer_norm(merged)
    coarse_queries = project(coarse_normed, coarse_inputs[:, : 2 * channels])
    coarse_pairs = project(coarse_normed, coarse_inputs[:, 2 * channels :])
    coarse_admit = (
        admit_mask.reshape(lat_rows // 2, 2, lon_cols // 2, 2).max(axis=(1, 3)).astype(jnp.float32)
    )
    coarse_mixed = attend(coarse_queries, coarse_pairs, coarse_admit, COARSE_HEADS)
    coarse_tokens = (
        merged + jnp.dot(coarse_mixed, coarse_output, preferred_element_type=jnp.float32)
    ).astype(jnp.bfloat16)
    return (skip_tokens, coarse_tokens)


def solution(mesh):
    return jax.shard_map(
        local,
        mesh=mesh,
        in_specs=(P(None, "lat", "lon", None), P("lat", "lon"), P("lon"), P("lon")),
        out_specs=(P(None, "lat", "lon", None), P(None, "lat", "lon", None)),
        check_vma=False,
    )
```

profile of v0, /device:TPU:6, one launch (start us, length us, event | category | flops | bytes accessed | tf_op | source)
XLA Modules:
  0.0 1260.2 jit_solution(13074116917296193016)
XLA Ops:
  7.2 0.7 all-gather.3.cloned.1.call-update
  7.9 0.7 all-gather.5.cloned.1.call-update
  8.6 0.7 convert_bitcast_fusion
  9.4 2.7 collective-permute-start.1
  12.1 1.9 collective-permute-start
  14.0 0.8 reshape.296
  15.1 1.1 convert_reduce_fusion
  16.2 1.2 fusion.37
  17.4 0.7 fusion.48
  18.1 0.4 collective-permute-done
  18.5 582.4 %all-gather.3.cloned.1.call-done = bf16[1048576]{0:T(1024)(128)(2,1)} async-done(((bf16[8192]{0:T(1024)(128)(2,1)}), bf16[1048576]{0:T(1024)(128)(2,1)}) %all-gather.3.cloned.1.call-update) | async-done | bytes 2097168 | tf_op jit(solution)/shard_map/all_gather | solution.py:93
  600.9 1.4 slice-done.1
  602.4 2.7 reshape.289
  605.0 1.7 fusion.26
  606.8 2.1 collective-permute-start.5
  608.9 2.4 collective-permute-start.4
  611.4 5.8 collective-permute-start.3
  617.1 1.9 collective-permute-start.2
  619.1 0.9 pad_maximum_fusion.3
  620.0 8.1 collective-permute-start.7
  628.2 2.1 collective-permute-start.6
  630.6 1.1 reshape.312
  631.7 1.4 fusion.31
  633.3 0.7 reshape.290
  634.1 2.1 copy.51
  636.2 8.1 collective-permute-done.6
  644.3 1.8 pad_maximum_fusion
  646.1 3.1 reshape.291
  649.2 2.4 copy.50
  651.6 3.4 copy.52
  655.0 16.4 %while.3 = (s32[]{:T(128)}, bf16[3,3,8,72,64]{3,4,2,1,0:T(8,128)(2,1)}, f32[3,3,72]{2,1,0:T(4,128)S(1)}, bf16[3,3,8,72,64]{3,4,2,1,0:T(8,128)(2,1)}, bf16[3,3,2,8,72,64]{4,5,3,1,2,0:T(8,128)(2,1)}, /*index=5*/s32[]{:T(128)}) while((s32[]{:T(128)}, bf16[3,3,8,72,64]{3,4,2,1,0:T(8,128)(2,1)}, f32[3,3,72]{2,1,0:T(4,128)S(1)}, ...), condition=%wide.region_5.6_spmd.clone, body=%wide.region_2.5_spmd.clone.sunk | while | flops 49028904 | bytes 5612977 | solution.py:80
  655.2 1.2 dynamic-slice_bitcast_fusion.2
  656.4 1.5 fusion.86
  657.9 1.4 fusion.87
  659.4 1.1 fusion.88
  660.6 1.2 dynamic-slice_bitcast_fusion.2
  661.8 1.6 fusion.86
  663.4 1.4 fusion.87
  664.8 1.1 fusion.88
  666.1 1.2 dynamic-slice_bitcast_fusion.2
  667.3 1.6 fusion.86
  668.8 1.4 fusion.87
  670.3 1.1 fusion.88
  671.4 2.6 copy.53
  674.1 0.9 reshape.294
  675.3 0.4 reshape.309
  676.1 0.5 copy.55
  676.5 0.5 reshape.306
  677.3 0.5 multiply_reduce_fusion
  677.8 532.3 %all-gather.5.cloned.1.call-done = bf16[6291456]{0:T(1024)(128)(2,1)} async-done(((bf16[49152]{0:T(1024)(128)(2,1)}), bf16[6291456]{0:T(1024)(128)(2,1)}) %all-gather.5.cloned.1.call-update) | async-done | bytes 12582928 | tf_op jit(solution)/shard_map/all_gather | solution.py:116
  1210.2 3.7 slice.136
  1213.8 7.3 reshape.313
  1221.2 6.4 slice.137
  1227.6 10.3 reshape.297
  1237.9 3.3 fusion.63
  1241.4 0.6 copy-done
  1242.0 0.5 fusion.32
  1242.5 0.9 fusion.22
  1243.6 0.6 reshape.300
  1244.8 0.4 fusion.64
  1245.2 0.4 fusion.25
  1246.7 1.6 slice-done
  1248.3 2.3 reshape.316
  1250.6 2.7 fusion.34
  (70 shorter events, 4.5 us)
Async XLA Ops:
  7.2 593.8 %all-gather.3.cloned.1.call-start = ((), (), s32[]{:S(2)}) async-start(), calls=%async_computation | async-start | bytes 2113536 | tf_op jit(solution)/shard_map/all_gather | solution.py:93
  7.9 1202.3 %all-gather.5.cloned.1.call-start = ((), (), s32[]{:S(2)}) async-start(), calls=%async_computation.1 | async-start | bytes 12681216 | tf_op jit(solution)/shard_map/all_gather | solution.py:116
  9.4 8.7 collective-permute-start.1
  12.1 6.4 collective-permute-start
  600.9 1.4 slice-start.1
  602.4 2.7 copy-start.1
  606.8 23.8 %slice-start.2 = ((bf16[1048576]{0:T(1024)(128)(2,1)}), bf16[262144]{0:T(1024)(128)(2,1)S(1)}, s32[]{:S(2)}) async-start(bf16[1048576]{0:T(1024)(128)(2,1)} %all-gather.3.cloned.1.call-done), calls=%async_computation.4 | async-start | bytes 1048576 | tf_op jit(solution)/shard_map/slice | solution.py:95
  606.8 12.3 collective-permute-start.5
  608.9 10.2 collective-permute-start.4
  611.4 18.9 %collective-permute-start.3 = (bf16[1,18,6]{2,1,0:T(8,128)(2,1)S(1)}, bf16[1,18,6]{2,1,0:T(8,128)(2,1)S(1)}, u32[]{:S(2)}, u32[]{:S(2)}) collective-permute-start(bf16[1,18,6]{2,1,0:T(8,128)(2,1)S(1)} %get-tuple-element.97), channel_id=1, source_target_pairs={{4,0},{8,4},{12,8},{16,12},{20,16},{24,20},{28,24},{32,28},{36,32}... | collective-permute-start | bytes 656 | tf_op jit(solution)/shard_map/ppermute | solution.py:27
  617.1 13.2 %collective-permute-start.2 = (bf16[1,18,6]{2,1,0:T(8,128)(2,1)S(1)}, bf16[1,18,6]{2,1,0:T(8,128)(2,1)S(1)}, u32[]{:S(2)}, u32[]{:S(2)}) collective-permute-start(bf16[1,18,6]{2,1,0:T(8,128)(2,1)S(1)} %get-tuple-element.96), channel_id=1, source_target_pairs={{0,4},{4,8},{8,12},{12,16},{16,20},{20,24},{24,28},{28,32},{32,36}... | collective-permute-start | bytes 656 | tf_op jit(solution)/shard_map/ppermute | solution.py:25
  619.1 12.6 %copy-start.2 = (bf16[1,3,24,1024]{3,2,1,0:T(8,128)(2,1)}, bf16[1,3,24,1024]{3,2,1,0:T(8,128)(2,1)S(1)}, u32[]{:S(2)}) copy-start(bf16[1,3,24,1024]{3,2,1,0:T(8,128)(2,1)S(1)} %collective-permute-done.5) | copy-start | bytes 442372
  619.1 12.6 %copy-start.4 = (bf16[1,3,24,1024]{3,2,1,0:T(8,128)(2,1)}, bf16[1,3,24,1024]{3,2,1,0:T(8,128)(2,1)S(1)}, u32[]{:S(2)}) copy-start(bf16[1,3,24,1024]{3,2,1,0:T(8,128)(2,1)S(1)} %collective-permute-done.4) | copy-start | bytes 442372
  620.0 16.1 %collective-permute-start.7 = (bf16[1,18,6,1024]{3,2,1,0:T(8,128)(2,1)}, bf16[1,18,6,1024]{3,2,1,0:T(8,128)(2,1)}, u32[]{:S(2)}, u32[]{:S(2)}) collective-permute-start(bf16[1,18,6,1024]{3,2,1,0:T(8,128)(2,1)} %get-tuple-element.91), channel_id=1, source_target_pairs={{4,0},{8,4},{12,8},{16,12},{20,16},{24,20},{28,24},{32,28},{36,32}... | collective-permute-start | bytes 663560 | tf_op jit(solution)/shard_map/ppermute | solution.py:27
  628.2 16.1 %collective-permute-start.6 = (bf16[1,18,6,1024]{3,2,1,0:T(8,128)(2,1)}, bf16[1,18,6,1024]{3,2,1,0:T(8,128)(2,1)}, u32[]{:S(2)}, u32[]{:S(2)}) collective-permute-start(bf16[1,18,6,1024]{3,2,1,0:T(8,128)(2,1)} %get-tuple-element.90), channel_id=1, source_target_pairs={{0,4},{4,8},{8,12},{12,16},{16,20},{20,24},{24,28},{28,32},{32,36}... | collective-permute-start | bytes 663560 | tf_op jit(solution)/shard_map/ppermute | solution.py:25
  634.1 10.2 copy-start.3
  634.1 10.2 copy-start.5
  674.0 1.0 copy-start.6
  675.3 0.7 copy-start.7
  1237.9 4.0 copy-start
  1243.4 1.4 copy-start.8
  1246.7 1.6 slice-start
Sparse Core Ops, SparseCore 0:
  10.1 590.8 all-gather.2
  603.0 607.0 all-gather.4
where the time goes:
time: 1260 us
  waiting for transfers between devices  1120 us (89%)
  local copies, waits for them, and re-layouts  61.5 us (5%)
  starting transfers between devices  27.1 us (2%)
  matrix products  24.3 us (2%)
  between operations  14.5 us (1%)
    all_gather x1, waiting for transfers between devices, local(): fine_flat = lax.all_gather(fine_params, 'lon', axis=0, tiled=True)  582 us
    all_gather x1, waiting for transfers between devices, local(): coarse_flat = lax.all_gather(coarse_params, 'lon', axis=0, tiled=True)  532 us
  transfers between devices with their start and end apart: 10, of which 4 were waited for; matrix products, arithmetic and copies ran while one was open for 4% of the time, Pallas kernels for 0%

commit v1 on v0

--- a/solution.py
+++ b/solution.py
@@ -3,6 +3,7 @@
 import jax
 import jax.numpy as jnp
 from jax import lax
+from jax.sharding import Mesh
 from jax.sharding import PartitionSpec as P
 
 FINE_HEADS = 8
@@ -12,6 +13,8 @@
 
 
 epsilon = 1e-05
+LON = ("xl", "y", "z")
+LAT = ("xh", "c")
 
 
 def with_halo(cells, sides, width, closed):
@@ -83,6 +86,17 @@
     return blended.reshape(levels, row_count, col_count, channels)
 
 
+def gather_params(fine_params, coarse_params):
+    fine_count = fine_params.shape[0]
+    width = 1024
+    packed = jnp.concatenate([fine_params, coarse_params]).reshape(-1, width)
+    pair = lax.all_gather(packed, "xl", axis=0, tiled=False)
+    every = lax.all_gather(pair, ("y", "z"), axis=0, tiled=False)
+    every = every.transpose(1, 0, 2, 3).reshape(-1, *packed.shape)
+    fine_rows = fine_count // width
+    return every[:, :fine_rows].reshape(-1), every[:, fine_rows:].reshape(-1)
+
+
 def local(latent, admit_mask, fine_params, coarse_params):
     channels = latent.shape[-1]
     levels = latent.shape[0]
@@ -90,7 +104,7 @@
     lat_rows, lon_cols = admit_mask.shape
     rim_lat = WIN_LAT // 2
     rim_lon = WIN_LON // 2
-    fine_flat = lax.all_gather(fine_params, "lon", axis=0, tiled=True)
+    fine_flat, coarse_flat = gather_params(fine_params, coarse_params)
     fine_inputs = fine_flat[: 3 * square].reshape(channels, 3 * channels)
     fine_output = fine_flat[3 * square :].reshape(channels, channels)
     normed = layer_norm(latent)
@@ -98,12 +112,12 @@
     outgoing = project(normed, fine_inputs[:, channels:])
     admitted = admit_mask.astype(jnp.bfloat16)[None]
     outgoing, admitted = (
-        with_halo(outgoing, (("lat", 1),), rim_lat, False),
-        with_halo(admitted, (("lat", 1),), rim_lat, False),
+        with_halo(outgoing, ((LAT, 1),), rim_lat, False),
+        with_halo(admitted, ((LAT, 1),), rim_lat, False),
     )
     outgoing, admitted = (
-        with_halo(outgoing, (("lon", 2),), rim_lon, True),
-        with_halo(admitted, (("lon", 2),), rim_lon, True),
+        with_halo(outgoing, ((LON, 2),), rim_lon, True),
+        with_halo(admitted, ((LON, 2),), rim_lon, True),
     )
     padding = ((0, 0), (rim_lat, rim_lat), (rim_lon, rim_lon), (0, 0))
     blended = attend(
@@ -113,7 +127,6 @@
     skip_tokens = (
         latent + jnp.dot(blended, fine_output, preferred_element_type=jnp.float32)
     ).astype(jnp.bfloat16)
-    coarse_flat = lax.all_gather(coarse_params, "lon", axis=0, tiled=True)
     coarse_merge = coarse_flat[: 8 * square].reshape(4 * channels, 2 * channels)
     coarse_inputs = coarse_flat[8 * square : 20 * square].reshape(2 * channels, 6 * channels)
     coarse_output = coarse_flat[20 * square :].reshape(2 * channels, 2 * channels)
@@ -136,10 +149,11 @@
 
 
 def solution(mesh):
+    split = Mesh(mesh.devices.reshape(2, 8, 8, 2, 2), (*LON, *LAT))
     return jax.shard_map(
         local,
-        mesh=mesh,
-        in_specs=(P(None, "lat", "lon", None), P("lat", "lon"), P("lon"), P("lon")),
-        out_specs=(P(None, "lat", "lon", None), P(None, "lat", "lon", None)),
+        mesh=split,
+        in_specs=(P(None, LAT, LON, None), P(LAT, LON), P(LON), P(LON)),
+        out_specs=(P(None, LAT, LON, None), P(None, LAT, LON, None)),
         check_vma=False,
     )

time: 1260 us -> 287 us (0.23)
  waiting for transfers between devices: 1120 us -> 125 us
  local copies, waits for them, and re-layouts: 61.5 us -> 75.3 us
    all_gather x2 -> x1, waiting for transfers between devices: 1110 us -> 123 us  [gather_params(): every = lax.all_gather(pair, ('y', 'z'), axis=0, tiled=False)]
    unnamed x22 -> x27, local copies, waits for them, and re-layouts: 7.1 us -> 20 us
  transfers between devices with their start and end apart: 10 -> 9, of which waited for: 4 -> 2; matrix products, arithmetic and copies ran while one was open for 4% -> 16% of each run, Pallas kernels for 0% -> 0%
where the time goes in v1:
time: 287 us; the launch traced here: 282 us
  waiting for transfers between devices  125 us (44%)
  local copies, waits for them, and re-layouts  75.3 us (26%)
  starting transfers between devices  26.5 us (9%)
  matrix products  25.2 us (9%)
  between operations  14.5 us (5%)
  other arithmetic  8.87 us (3%)
  blocking collectives  5.67 us (2%)
    all_gather x1, waiting for transfers between devices, gather_params(): every = lax.all_gather(pair, ('y', 'z'), axis=0, tiled=False)  123 us
    unnamed x27, local copies, waits for them, and re-layouts  20 us
    ppermute x4, starting transfers between devices, with_halo(): lax.ppermute(head, axis, [((i + 1) % count, i) for i in range(ends)])  18.3 us
    slice x1, local copies, waits for them, and re-layouts, gather_params(): return (every[:, :fine_rows].reshape(-1), every[:, fine_rows:].reshape(-1))  11 us
    reshape x1, local copies, waits for them, and re-layouts, local(): coarse_flat[8 * square:20 * square].reshape(2 * channels, 6 * channels)  10.3 us
    dot_general x5, matrix products, project(): jnp.dot(values, matrix, preferred_element_type=jnp.float32)  8.72 us
    reshape x7, local copies, waits for them, and re-layouts, windows(): values.reshape(levels, win_rows, WIN_LAT, win_cols, WIN_LON, segments, he...  8.17 us
    ppermute x4, starting transfers between devices, with_halo(): lax.ppermute(tail, axis, [(i, (i + 1) % count) for i in range(ends)])  8.17 us
  transfers between devices with their start and end apart: 9, of which 2 were waited for; matrix products, arithmetic and copies ran while one was open for 16% of the time, Pallas kernels for 0%

profile of v1, /device:TPU:6, one launch (start us, length us, event | category | flops | bytes accessed | tf_op | source)
XLA Modules:
  0.0 281.7 jit_solution(13602505429083771550)
XLA Ops:
  7.2 0.9 pad_maximum_fusion.4
  8.2 5.7 %all_gather.9 = bf16[2,56,1024]{2,1,0:T(8,128)(2,1)} all-gather(bf16[1,56,1024]{2,1,0:T(8,128)(2,1)S(1)} %all_gather_reshape.3), channel_id=1, replica_groups=mesh['xl'=2,'y'=8,'z'=8,'xh'=2,'c'=2] {'xl'}, dimensions={0}, use_global_device_ids=true | all-gather | bytes 344064 | tf_op jit(solution)/shard_map/all_gather | solution.py:93
  13.9 0.7 convert_bitcast_fusion
  14.6 1.9 collective-permute-start.1
  16.5 2.4 collective-permute-start
  18.9 0.8 reshape.291
  20.0 1.1 convert_reduce_fusion
  21.1 1.2 fusion.41
  22.3 0.7 fusion.52
  23.0 2.0 collective-permute-done
  24.9 123.4 %all-gather.3.cloned.1.call-done = bf16[128,56,1024]{2,1,0:T(8,128)(2,1)} async-done(((bf16[2,56,1024]{2,1,0:T(8,128)(2,1)}), bf16[128,56,1024]{2,1,0:T(8,128)(2,1)}) %all-gather.3.cloned.1.call-update) | async-done | bytes 14680080 | tf_op jit(solution)/shard_map/all_gather | solution.py:94
  148.4 7.4 %copy.50 = bf16[2,64,56,1024]{3,2,1,0:T(8,128)(2,1)S(1)} copy(bf16[2,64,56,1024]{3,2,0,1:T(8,128)(2,1)} %bitcast.158) | data formatting | bytes 29360128 | tf_op jit(solution)/shard_map/transpose | solution.py:95
  155.8 5.2 %copy-done = bf16[2,64,56,1024]{3,2,1,0:T(8,128)(2,1)} copy-done((bf16[2,64,56,1024]{3,2,1,0:T(8,128)(2,1)}, bf16[2,64,56,1024]{3,2,1,0:T(8,128)(2,1)S(1)}, u32[]{:S(2)}) %copy-start) | copy-done | bytes 14680088
  161.2 1.8 reshape.283
  163.0 1.7 fusion.28
  164.8 2.8 collective-permute-start.5
  167.6 1.9 collective-permute-start.4
  169.6 5.5 %collective-permute-start.3 = (bf16[1,18,6]{2,1,0:T(8,128)(2,1)S(1)}, bf16[1,18,6]{2,1,0:T(8,128)(2,1)S(1)}, u32[]{:S(2)}, u32[]{:S(2)}) collective-permute-start(bf16[1,18,6]{2,1,0:T(8,128)(2,1)S(1)} %get-tuple-element.97), channel_id=1, source_target_pairs={{4,0},{8,4},{12,8},{16,12},{20,16},{24,20},{28,24},{32,28},{36,32}... | collective-permute-start | bytes 656 | tf_op jit(solution)/shard_map/ppermute | solution.py:30
  175.1 1.9 collective-permute-start.2
  177.1 0.6 copy-done.2
  177.7 0.9 pad_maximum_fusion.3
  178.7 8.1 %collective-permute-start.7 = (bf16[1,18,6,1024]{3,2,1,0:T(8,128)(2,1)}, bf16[1,18,6,1024]{3,2,1,0:T(8,128)(2,1)}, u32[]{:S(2)}, u32[]{:S(2)}) collective-permute-start(bf16[1,18,6,1024]{3,2,1,0:T(8,128)(2,1)} %get-tuple-element.91), channel_id=1, source_target_pairs={{4,0},{8,4},{12,8},{16,12},{20,16},{24,20},{28,24},{32,28},{36,32}... | collective-permute-start | bytes 663560 | tf_op jit(solution)/shard_map/ppermute | solution.py:30
  186.8 1.9 collective-permute-start.6
  189.0 1.1 slice.116
  190.1 11.0 %slice.117 = bf16[128,48,1024]{2,1,0:T(8,128)(2,1)} slice(bf16[128,56,1024]{2,1,0:T(8,128)(2,1)} %bitcast.156), slice={[0:128], [8:56], [0:1024]} | slice | bytes 25165824 | tf_op jit(solution)/shard_map/slice | solution.py:97
  201.1 1.0 reshape.309
  202.1 1.4 fusion.34
  203.6 0.7 reshape.284
  204.4 2.1 copy.53
  206.5 7.8 %copy.69 = bf16[768,8,8,128]{3,1,2,0:T(8,128)(2,1)S(1)} copy(bf16[768,8,8,128]{3,2,1,0:T(8,128)(2,1)} %bitcast.151) | data formatting | bytes 25165824
  214.3 2.9 %slice.119 = bf16[3145728]{0:T(1024)(128)(2,1)} slice(bf16[6291456]{0:T(1024)(128)(2,1)S(1)} %bitcast.157), slice={[2097152:5242880]} | slice | bytes 12582912 | tf_op jit(solution)/shard_map/slice | solution.py:131
  217.2 10.3 %reshape.293 = bf16[1024,3072]{1,0:T(8,128)(2,1)} reshape(bf16[3145728]{0:T(1024)(128)(2,1)} %slice.119) | data formatting | bytes 12582912 | tf_op jit(solution)/shard_map/reshape | solution.py:131
  227.6 1.8 pad_maximum_fusion
  229.4 3.1 %reshape.285 = bf16[1,3,6,3,12,2,8,64]{7,6,5,4,3,2,1,0:T(8,128)(2,1)} reshape(bf16[1,18,36,1024]{3,2,1,0:T(8,128)(2,1)S(1)} %pad_maximum_fusion) | data formatting | bytes 2654208 | tf_op jit(solution)/shard_map/reshape | solution.py:56
  232.5 2.4 copy.52
  234.9 3.5 %copy.54 = bf16[3,3,2,8,72,64]{4,5,3,1,2,0:T(8,128)(2,1)} copy(bf16[3,3,2,8,72,64]{5,3,4,2,1,0:T(8,128)(2,1)S(1)} %bitcast.159) | data formatting | bytes 2654208
  238.4 16.4 %while.3 = (s32[]{:T(128)}, bf16[3,3,8,72,64]{3,4,2,1,0:T(8,128)(2,1)}, f32[3,3,72]{2,1,0:T(4,128)S(1)}, bf16[3,3,8,72,64]{3,4,2,1,0:T(8,128)(2,1)}, bf16[3,3,2,8,72,64]{4,5,3,1,2,0:T(8,128)(2,1)}, /*index=5*/s32[]{:T(128)}) while((s32[]{:T(128)}, bf16[3,3,8,72,64]{3,4,2,1,0:T(8,128)(2,1)}, f32[3,3,72]{2,1,0:T(4,128)S(1)}, ...), condition=%wide.region_5.6_spmd.clone, body=%wide.region_2.5_spmd.clone.sunk | while | flops 49028904 | bytes 5612977 | solution.py:83
  238.5 1.2 dynamic-slice_bitcast_fusion.2
  239.7 1.5 fusion.88
  241.2 1.4 fusion.89
  242.7 1.1 fusion.90
  243.9 1.2 dynamic-slice_bitcast_fusion.2
  245.1 1.6 fusion.88
  246.7 1.4 fusion.89
  248.1 1.1 fusion.90
  249.4 1.2 dynamic-slice_bitcast_fusion.2
  250.6 1.5 fusion.88
  252.1 1.4 fusion.89
  253.6 1.1 fusion.90
  254.7 2.7 copy.55
  257.6 0.9 reshape.288
  258.5 0.3 fusion.31
  258.8 0.4 reshape.305
  259.6 0.5 copy.57
  260.0 1.4 reshape.302
  261.4 0.5 multiply_reduce_fusion
  262.0 3.5 %fusion.67 = (f32[6,12]{1,0:T(8,128)S(1)}, f32[6,12,1024]{2,1,0:T(8,128)S(1)}) fusion(bf16[6144,1024]{1,0:T(8,128)(2,1)} %bitcast.152, f32[6,12,2048]{2,1,0:T(8,128)} %reshape.302, f32[6,12]{1,0:T(8,128)S(1)} %add_rsqrt_fusion.2, f32[6,12]{1,0:T(8,128)S(1)} %broadcast_multiply_fusion.2), kind=kOutput, calls=%fused_computation.100 | convolution fusion | flops 302653376 | bytes 5276512 | tf_op jit(solution)/shard_map/dot_general | solution.py:45
  265.7 1.2 fusion.35
  266.9 0.9 fusion.23
  267.8 1.2 reshape.294
  269.0 0.6 reshape.296
  270.2 0.4 fusion.68
  270.6 0.4 fusion.27
  272.1 2.7 fusion.38
  (71 shorter events, 3.8 us)
Async XLA Ops:
  7.2 141.2 %all-gather.3.cloned.1.call-start = ((), (), s32[]{:S(2)}) async-start(), calls=%async_computation | async-start | bytes 14909440 | tf_op jit(solution)/shard_map/all_gather | solution.py:94
  14.6 8.4 %collective-permute-start.1 = (bf16[1,3,24]{2,1,0:T(4,128)(2,1)S(1)}, bf16[1,3,24]{2,1,0:T(4,128)(2,1)S(1)}, u32[]{:S(2)}, u32[]{:S(2)}) collective-permute-start(bf16[1,3,24]{2,1,0:T(4,128)(2,1)S(1)} %get-tuple-element.99), channel_id=1, source_target_pairs={{1,0},{2,1},{3,2},{5,4},{6,5},{7,6},{9,8},{10,9},{11,10},{13,12},{... | collective-permute-start | bytes 440 | tf_op jit(solution)/shard_map/ppermute | solution.py:30
  16.5 8.4 %collective-permute-start = (bf16[1,3,24]{2,1,0:T(4,128)(2,1)S(1)}, bf16[1,3,24]{2,1,0:T(4,128)(2,1)S(1)}, u32[]{:S(2)}, u32[]{:S(2)}) collective-permute-start(bf16[1,3,24]{2,1,0:T(4,128)(2,1)S(1)} %get-tuple-element.98), channel_id=1, source_target_pairs={{0,1},{1,2},{2,3},{4,5},{5,6},{6,7},{8,9},{9,10},{10,11},{12,13},{... | collective-permute-start | bytes 440 | tf_op jit(solution)/shard_map/ppermute | solution.py:28
  155.8 5.2 %copy-start = (bf16[2,64,56,1024]{3,2,1,0:T(8,128)(2,1)}, bf16[2,64,56,1024]{3,2,1,0:T(8,128)(2,1)S(1)}, u32[]{:S(2)}) copy-start(bf16[2,64,56,1024]{3,2,1,0:T(8,128)(2,1)S(1)} %copy.50) | copy-start | bytes 44040196
  161.2 1.8 copy-start.1
  164.8 12.3 %collective-permute-start.5 = (bf16[1,3,24,1024]{3,2,1,0:T(8,128)(2,1)S(1)}, bf16[1,3,24,1024]{3,2,1,0:T(8,128)(2,1)S(1)}, u32[]{:S(2)}, u32[]{:S(2)}) collective-permute-start(bf16[1,3,24,1024]{3,2,1,0:T(8,128)(2,1)S(1)} %get-tuple-element.95), channel_id=1, source_target_pairs={{1,0},{2,1},{3,2},{5,4},{6,5},{7,6},{9,8},{10,9},{11,10},{13,12},{... | collective-permute-start | bytes 442376 | tf_op jit(solution)/shard_map/ppermute | solution.py:30
  167.6 9.5 %collective-permute-start.4 = (bf16[1,3,24,1024]{3,2,1,0:T(8,128)(2,1)S(1)}, bf16[1,3,24,1024]{3,2,1,0:T(8,128)(2,1)S(1)}, u32[]{:S(2)}, u32[]{:S(2)}) collective-permute-start(bf16[1,3,24,1024]{3,2,1,0:T(8,128)(2,1)S(1)} %get-tuple-element.94), channel_id=1, source_target_pairs={{0,1},{1,2},{2,3},{4,5},{5,6},{6,7},{8,9},{9,10},{10,11},{12,13},{... | collective-permute-start | bytes 442376 | tf_op jit(solution)/shard_map/ppermute | solution.py:28
  169.6 19.1 %collective-permute-start.3 = (bf16[1,18,6]{2,1,0:T(8,128)(2,1)S(1)}, bf16[1,18,6]{2,1,0:T(8,128)(2,1)S(1)}, u32[]{:S(2)}, u32[]{:S(2)}) collective-permute-start(bf16[1,18,6]{2,1,0:T(8,128)(2,1)S(1)} %get-tuple-element.97), channel_id=1, source_target_pairs={{4,0},{8,4},{12,8},{16,12},{20,16},{24,20},{28,24},{32,28},{36,32}... | collective-permute-start | bytes 656 | tf_op jit(solution)/shard_map/ppermute | solution.py:30
  175.1 13.6 %collective-permute-start.2 = (bf16[1,18,6]{2,1,0:T(8,128)(2,1)S(1)}, bf16[1,18,6]{2,1,0:T(8,128)(2,1)S(1)}, u32[]{:S(2)}, u32[]{:S(2)}) collective-permute-start(bf16[1,18,6]{2,1,0:T(8,128)(2,1)S(1)} %get-tuple-element.96), channel_id=1, source_target_pairs={{0,4},{4,8},{8,12},{12,16},{16,20},{20,24},{24,28},{28,32},{32,36}... | collective-permute-start | bytes 656 | tf_op jit(solution)/shard_map/ppermute | solution.py:28
  177.1 0.7 copy-start.2
  177.7 0.9 copy-start.4
  178.7 48.9 %collective-permute-start.7 = (bf16[1,18,6,1024]{3,2,1,0:T(8,128)(2,1)}, bf16[1,18,6,1024]{3,2,1,0:T(8,128)(2,1)}, u32[]{:S(2)}, u32[]{:S(2)}) collective-permute-start(bf16[1,18,6,1024]{3,2,1,0:T(8,128)(2,1)} %get-tuple-element.91), channel_id=1, source_target_pairs={{4,0},{8,4},{12,8},{16,12},{20,16},{24,20},{28,24},{32,28},{36,32}... | collective-permute-start | bytes 663560 | tf_op jit(solution)/shard_map/ppermute | solution.py:30
  186.8 40.8 %collective-permute-start.6 = (bf16[1,18,6,1024]{3,2,1,0:T(8,128)(2,1)}, bf16[1,18,6,1024]{3,2,1,0:T(8,128)(2,1)}, u32[]{:S(2)}, u32[]{:S(2)}) collective-permute-start(bf16[1,18,6,1024]{3,2,1,0:T(8,128)(2,1)} %get-tuple-element.90), channel_id=1, source_target_pairs={{0,4},{4,8},{8,12},{12,16},{16,20},{20,24},{24,28},{28,32},{32,36}... | collective-permute-start | bytes 663560 | tf_op jit(solution)/shard_map/ppermute | solution.py:28
  217.2 10.4 %copy-start.3 = (bf16[1,3,24,1024]{3,2,1,0:T(8,128)(2,1)S(1)}, bf16[1,3,24,1024]{3,2,1,0:T(8,128)(2,1)}, u32[]{:S(2)}) copy-start(bf16[1,3,24,1024]{3,2,1,0:T(8,128)(2,1)} %copy-done.2) | copy-start | bytes 442372
  217.2 10.4 %copy-start.5 = (bf16[1,3,24,1024]{3,2,1,0:T(8,128)(2,1)S(1)}, bf16[1,3,24,1024]{3,2,1,0:T(8,128)(2,1)}, u32[]{:S(2)}) copy-start(bf16[1,3,24,1024]{3,2,1,0:T(8,128)(2,1)} %copy-done.4) | copy-start | bytes 442372
  257.5 1.0 copy-start.6
  258.8 0.7 copy-start.7
  260.0 5.7 %slice-start = ((s8[6291456]{0:T(1024)(128)(4,1)}), s8[2097152]{0:T(1024)(128)(4,1)S(1)}, s32[]{:S(2)}) async-start(s8[6291456]{0:T(1024)(128)(4,1)} %bitcast.161), calls=%async_computation.1 | async-start | bytes 4194304
  262.0 3.7 %slice-start.1 = ((s8[6291456]{0:T(1024)(128)(4,1)}), s8[4194304]{0:T(1024)(128)(4,1)S(1)}, s32[]{:S(2)}) async-start(s8[6291456]{0:T(1024)(128)(4,1)} %bitcast.161), calls=%async_computation.2 | async-start | bytes 8388608
  267.8 2.4 copy-start.8
Sparse Core Ops, SparseCore 0:
  14.0 134.3 all-gather.2

commit v2 on v1

v2 whole, which is shorter than its diff:
```python
import math

import jax
import jax.numpy as jnp
import numpy as np
from jax import lax
from jax.experimental import pallas as pl
from jax.experimental.pallas import tpu as pltpu
from jax.sharding import Mesh
from jax.sharding import PartitionSpec as P

FINE_HEADS = 8
COARSE_HEADS = 16
HEAD = 64
WIN_LAT = 6
WIN_LON = 12
LON = ("xl", "y", "z")
LAT = ("xh", "c")

epsilon = 1e-05

ROWS, COLS = 12, 24
WIN = WIN_LAT * WIN_LON
WIN_PAD = 80
CELL_PAD = 16
COARSE_PAD = WIN_LAT * CELL_PAD
CELLS = 4 * COARSE_PAD
GROUP = 4


def token_orders():
    top, side = WIN_LAT // 2, WIN_LON // 2
    own = ROWS * COLS
    high = ROWS + 2 * top

    def source(row, col):
        if col < side:
            return own + 2 * top * COLS + row * side + col
        if col >= side + COLS:
            return own + 2 * top * COLS + high * side + row * side + col - side - COLS
        col -= side
        if row < top:
            return own + row * COLS + col
        if row >= top + ROWS:
            return own + top * COLS + (row - top - ROWS) * COLS + col
        return (row - top) * COLS + col

    windows, counts, place = [], [], {}
    for a in range(high // WIN_LAT):
        for b in range((COLS + 2 * side) // WIN_LON):
            inner, outer = [], []
            for row in range(a * WIN_LAT, (a + 1) * WIN_LAT):
                for col in range(b * WIN_LON, (b + 1) * WIN_LON):
                    at = source(row, col)
                    (inner if at < own else outer).append(at)
            for k, at in enumerate(inner):
                place[at] = (len(counts), k)
            counts.append(-(-len(inner) // 16) * 16)
            windows.append(inner + outer + [-1] * (WIN_PAD - WIN))
    starts = np.concatenate([[0], np.cumsum(counts)])
    blended_at = {at: starts[w] + k for at, (w, k) in place.items()}
    cells = -np.ones((2, 2, WIN_LAT, CELL_PAD), np.int32)
    for row in range(ROWS):
        for col in range(COLS):
            cells[col % 2, row % 2, row // 2, col // 2] = row * COLS + col
    cells = cells.reshape(-1)
    from_blended = np.array([blended_at[c] if c >= 0 else -1 for c in cells], np.int32)
    back = np.zeros(own, np.int32)
    for k, c in enumerate(cells):
        if c >= 0:
            back[c] = k
    return np.array(windows, np.int32).reshape(-1), counts, cells, from_blended, back


WINDOWS, COUNTS, CELL_OF, FROM_BLENDED, BACK = token_orders()
SOURCES = ROWS * COLS + WIN_LAT * COLS + WIN_LON * (ROWS + WIN_LAT)


def one_hot(index, width):
    return (jnp.asarray(index)[:, None] == jnp.arange(width, dtype=jnp.int32)).astype(jnp.bfloat16)


def layer_norm(values):
    values = values.astype(jnp.float32)
    centered = values - jnp.mean(values, axis=-1, keepdims=True)
    spread = jnp.mean(centered * centered, axis=-1, keepdims=True)
    return (centered * lax.rsqrt(spread + epsilon)).astype(jnp.bfloat16)


def dot(left, right):
    return jnp.dot(left, right, preferred_element_type=jnp.float32)


def attend(queries, keys, values, bias):
    count = queries.shape[0]
    lane = lax.broadcasted_iota(jnp.int32, (1, GROUP * HEAD), 1) // HEAD
    spread = jnp.concatenate(
        [jnp.where(lane == h, queries, jnp.zeros_like(queries)) for h in range(GROUP)], axis=0
    )
    scores = lax.dot_general(
        spread, keys, (((1,), (1,)), ((), ())), preferred_element_type=jnp.float32
    )
    scores = scores * (1.0 / math.sqrt(HEAD)) + jnp.concatenate([bias] * GROUP, axis=0)
    raised = jnp.exp(scores - jnp.max(scores, axis=-1, keepdims=True))
    total = jnp.sum(raised, axis=-1, keepdims=True)
    mixed = dot(raised.astype(jnp.bfloat16), values) * (1.0 / total)
    out = jnp.where(lane == 0, mixed[:count], 0.0)
    for h in range(1, GROUP):
        out = jnp.where(lane == h, mixed[h * count : (h + 1) * count], out)
    return out.astype(jnp.bfloat16)


def fine_block(
    tokens, bias, cells, from_blended, back, weights, wide, queries, key_values, blended, skip, arrived
):
    channels = tokens.shape[1]
    width, lane = channels // 2, 128
    blocks = width // lane
    own = jnp.concatenate(
        [tokens[w * WIN_PAD : w * WIN_PAD + n] for w, n in enumerate(COUNTS)], axis=0
    )
    sides = []
    for c in range(2):
        arrived(c)
        side = weights[c].reshape(-1, width)
        sides.append(side)
        for b in range(blocks):
            wide[c * blocks + b] = side[: 3 * channels, b * lane : (b + 1) * lane].astype(
                jnp.float32
            )
        lanes = slice(c * width, (c + 1) * width)
        for j in range(3):
            matrix = jnp.concatenate(
                [
                    wide[c * blocks + b, pl.ds(j, channels, stride=3), :].astype(jnp.bfloat16)
                    for b in range(blocks)
                ],
                axis=1,
            )
            if j:
                key_values[j - 1, :, lanes] = dot(tokens[...], matrix).astype(jnp.bfloat16)
            else:
                queries[:, lanes] = dot(own, matrix).astype(jnp.bfloat16)
    start = 0
    span = GROUP * HEAD
    for w, count in enumerate(COUNTS):
        at = w * WIN_PAD
        for g in range(channels // span):
            lanes = slice(g * span, (g + 1) * span)
            blended[start : start + count, lanes] = attend(
                queries[start : start + count, lanes],
                key_values[0, at : at + WIN_PAD, lanes],
                key_values[1, at : at + WIN_PAD, lanes],
                bias[w, :count, :],
            )
        start += count
    ordered = dot(from_blended[...], blended[...]).astype(jnp.bfloat16)
    added = jnp.concatenate([dot(ordered, side[3 * channels :]) for side in sides], axis=1)
    tokens_out = (cells[...].astype(jnp.float32) + added).astype(jnp.bfloat16)
    skip[...] = dot(back[...], tokens_out).astype(jnp.bfloat16)
    joined = jnp.concatenate(
        [tokens_out[k * COARSE_PAD : (k + 1) * COARSE_PAD] for k in range(4)], axis=1
    )
    return layer_norm(joined)


def kernel(
    core,
    tokens,
    bias,
    cells,
    from_blended,
    back,
    coarse_bias,
    mine,
    other,
    skip,
    out,
    fine_weights,
    wide,
    queries,
    key_values,
    fine_blended,
    weights,
    spread,
    qkv,
    blended,
    fine_arrived,
    arrived,
):
    cores, pairs, ys, zs, fine_rows, block_width = fine_weights.shape
    blocks, rows = weights.shape[0], weights.shape[4]
    parts = blocks // cores
    channels = 2 * tokens.shape[1]

    def fine_copies(side, held):
        here = pl.ds(parts * rows, fine_rows)
        found = []
        for pair in range(pairs):
            for k in range(1 if side == 0 else zs):
                source = held.at[:, :, pair, here] if side == 0 else held.at[k, :, pair, here]
                target = fine_weights.at[side, pair]
                target = target if side == 0 else target.at[:, k]
                found.append(pltpu.make_async_copy(source, target, fine_arrived.at[side, pair, k]))
        return found

    def coarse_copies(side, held, pair):
        found = []
        for part in range(parts):
            here = pl.ds(part * rows, rows)
            for k in range(1 if side == 0 else zs):
                source = held.at[:, :, pair, here] if side == 0 else held.at[k, :, pair, here]
                target = weights.at[side * parts + part, pair]
                target = target if side == 0 else target.at[:, k]
                found.append(
                    pltpu.make_async_copy(source, target, arrived.at[side, pair, part, k])
                )
        return found

    def begin(start):
        @pl.when(core[0] == 0)
        def _():
            start((mine, other))

        @pl.when(core[0] != 0)
        def _():
            start((other, mine))

    def start_fine(held):
        for side in range(cores):
            for copy in fine_copies(side, held[side]):
                copy.start()

    def start_coarse(held):
        for pair in range(pairs):
            for side in range(cores):
                for copy in coarse_copies(side, held[side], pair):
                    copy.start(priority=1)

    def fine_wait(side):
        for copy in fine_copies(side, mine):
            copy.wait()
        if side == 0:
            begin(start_coarse)

    def wait(pair):
        for side in range(cores):
            for copy in coarse_copies(side, mine, pair):
                copy.wait()

    begin(start_fine)

    def times(left, first, last):
        sums = []
        for q in range(blocks):
            sums.append(dot(left, weights[q].reshape(-1, block_width)[first:last]))
        return jnp.concatenate(sums, axis=1)

    joined = fine_block(
        tokens,
        bias,
        cells,
        from_blended,
        back,
        fine_weights,
        wide,
        queries,
        key_values,
        fine_blended,
        skip,
        fine_wait,
    )
    merge_rows = 2 * channels
    wait(0)
    merged = times(joined, 0, merge_rows).astype(jnp.bfloat16)
    normed = layer_norm(merged)
    block = 128
    into = lax.broadcasted_iota(jnp.int32, (block, 9 * block), 1)
    places = (into // (3 * block)) + 3 * lax.broadcasted_iota(jnp.int32, (block, 9 * block), 0)
    places = (into % (3 * block) == places).astype(jnp.bfloat16)
    for b in range(channels // block):
        apart = dot(normed[:, b * block : (b + 1) * block], places).astype(jnp.bfloat16)
        for j in range(3):
            spread[j * COARSE_PAD : (j + 1) * COARSE_PAD, 3 * block * b : 3 * block * (b + 1)] = (
                apart[:, 3 * block * j : 3 * block * (j + 1)]
            )
    wait(1)
    qkv[...] = times(spread[...], merge_rows, merge_rows + 3 * channels).astype(jnp.bfloat16)
    span = GROUP * HEAD
    for g in range(channels // span):
        lanes = slice(g * span, (g + 1) * span)
        blended[:, lanes] = attend(
            qkv[:COARSE_PAD, lanes],
            qkv[COARSE_PAD : 2 * COARSE_PAD, lanes],
            qkv[2 * COARSE_PAD :, lanes],
            coarse_bias[...],
        )
    added = times(blended[...], merge_rows + 3 * channels, merge_rows + 4 * channels)
    result = (merged.astype(jnp.float32) + added).astype(jnp.bfloat16)
    out[...] = result.reshape(WIN_LAT, CELL_PAD, channels)[:, :WIN_LON]


VMEM = pl.BlockSpec(memory_space=pltpu.VMEM)


def run(core, tokens, bias, cells, coarse_bias, mine, other, fine_rows):
    outer, inner, pairs, packed_rows, block_width = mine.shape
    channels = tokens.shape[1]
    wider = 2 * channels
    cores, blocks = 2, wider // block_width
    rows = (packed_rows - fine_rows) * cores // blocks
    ys, zs = lax.axis_size("y"), lax.axis_size("z")
    hbm = pl.BlockSpec(memory_space=pltpu.HBM)
    return pl.pallas_call(
        kernel,
        out_shape=(
            jax.ShapeDtypeStruct((ROWS * COLS, channels), jnp.bfloat16),
            jax.ShapeDtypeStruct((WIN_LAT, WIN_LON, wider), jnp.bfloat16),
        ),
        in_specs=[pl.BlockSpec(memory_space=pltpu.SMEM)] + [VMEM] * 6 + [hbm] * 2,
        out_specs=(VMEM, VMEM),
        scratch_shapes=[
            pltpu.VMEM((cores, pairs, ys, zs, fine_rows, block_width), jnp.bfloat16),
            pltpu.VMEM((channels // 128, 3 * channels, 128), jnp.float32),
            pltpu.VMEM((sum(COUNTS), channels), jnp.bfloat16),
            pltpu.VMEM((2, tokens.shape[0], channels), jnp.bfloat16),
            pltpu.VMEM((sum(COUNTS), channels), jnp.bfloat16),
            pltpu.VMEM((blocks, pairs, ys, zs, rows, block_width), jnp.bfloat16),
            pltpu.VMEM((3 * COARSE_PAD, 3 * wider), jnp.bfloat16),
            pltpu.VMEM((3 * COARSE_PAD, wider), jnp.bfloat16),
            pltpu.VMEM((COARSE_PAD, wider), jnp.bfloat16),
            pltpu.SemaphoreType.DMA((cores, pairs, zs)),
            pltpu.SemaphoreType.DMA((cores, pairs, blocks // cores, zs)),
        ],
        compiler_params=pltpu.CompilerParams(vmem_limit_bytes=48 * 2**20),
        cost_estimate=pl.CostEstimate(
            flops=4 * 10**9, bytes_accessed=18 * 10**6, transcendentals=2 * 10**6
        ),
    )(
        core,
        tokens,
        bias,
        cells,
        one_hot(FROM_BLENDED, sum(COUNTS)),
        one_hot(BACK, CELLS),
        coarse_bias,
        mine,
        other,
    )


def neighbours(values, axes, dim, width, closed):
    count = lax.axis_size(axes)
    ends = count if closed else count - 1
    head = lax.slice_in_dim(values, 0, width, axis=dim)
    tail = lax.slice_in_dim(values, values.shape[dim] - width, values.shape[dim], axis=dim)
    before = lax.ppermute(tail, axes, [(i, (i + 1) % count) for i in range(ends)])
    after = lax.ppermute(head, axes, [((i + 1) % count, i) for i in range(ends)])
    return before, after


def gather_params(fine_params, coarse_params, channels):
    first = lax.axis_index("c") == 0
    quarter = channels // 2
    coarse = coarse_params.reshape(-1, 2 * channels)
    fine = fine_params.reshape(-1, channels)

    def columns(at):
        return [
            coarse[:, 2 * at * quarter : (2 * at + 1) * quarter],
            coarse[:, (2 * at + 1) * quarter : (2 * at + 2) * quarter],
            fine[:, at * quarter : (at + 1) * quarter],
        ]

    packed = jnp.where(
        first, jnp.concatenate(columns(0), axis=0), jnp.concatenate(columns(1), axis=0)
    )
    pair = lax.all_gather(packed, "xl", axis=0, tiled=False)
    ys, zs = lax.axis_size("y"), lax.axis_size("z")
    at = np.arange(2 * ys * zs).reshape(ys, zs, 2)
    along_y, along_z = [
        [at[:, z, c].tolist() for z in range(zs)] for c in range(2)
    ], [[at[y, :, c].tolist() for y in range(ys)] for c in range(2)]
    axes = ("y", "z", "c")
    held = lax.all_gather(pair, axes, axis_index_groups=along_z[0] + along_y[1])
    mine = lax.all_gather(held, axes, axis_index_groups=along_y[0] + along_z[1])
    return mine, fine.shape[0]


def local(latent, admit_mask, fine_params, coarse_params):
    channels = latent.shape[-1]
    mine, fine_rows = gather_params(fine_params, coarse_params, channels)

    extra = 128
    admitted = jnp.broadcast_to(
        admit_mask.astype(jnp.bfloat16)[:, :, None], (*admit_mask.shape, extra)
    )
    cells = jnp.concatenate([latent[0], admitted], axis=2)
    north, south = neighbours(cells, LAT, 0, WIN_LAT // 2, False)
    tall = jnp.concatenate([north, cells, south], axis=0)
    west, east = neighbours(tall, LON, 1, WIN_LON // 2, True)
    sources = jnp.concatenate(
        [v.reshape(-1, channels + extra) for v in (cells, north, south, west, east)], axis=0
    )
    placed = dot(one_hot(WINDOWS, SOURCES), sources)
    tokens = layer_norm(placed[:, :channels])
    fine_admit = placed[:, channels].reshape(-1, WIN_PAD)
    diagonal = jnp.eye(WIN_PAD, dtype=bool)
    fine_bias = jnp.where((fine_admit[:, None, :] > 0) | diagonal, 0.0, -jnp.inf)
    own = dot(one_hot(CELL_OF, ROWS * COLS), latent.reshape(-1, channels)).astype(jnp.bfloat16)

    coarse_admit = admit_mask.reshape(ROWS // 2, 2, COLS // 2, 2).max(axis=(1, 3))
    coarse_admit = jnp.pad(coarse_admit, ((0, 0), (0, CELL_PAD - COLS // 2))).reshape(1, -1)
    coarse_bias = jnp.where((coarse_admit > 0) | jnp.eye(COARSE_PAD, dtype=bool), 0.0, -jnp.inf)
    mine, tokens, fine_bias, own, coarse_bias = lax.optimization_barrier(
        (mine, tokens, fine_bias, own, coarse_bias)
    )
    other = lax.ppermute(mine, "c", [(0, 1), (1, 0)])
    core = lax.axis_index("c").reshape(1)
    skip, coarse = run(core, tokens, fine_bias, own, coarse_bias, mine, other, fine_rows)
    return skip.reshape(latent.shape), coarse[None]


def solution(mesh):
    split = Mesh(mesh.devices.reshape(2, 8, 8, 2, 2), (*LON, *LAT))
    return jax.shard_map(
        local,
        mesh=split,
        in_specs=(P(None, LAT, LON, None), P(LAT, LON), P(LON), P(LON)),
        out_specs=(P(None, LAT, LON, None), P(None, LAT, LON, None)),
        check_vma=False,
    )
```

time: 287 us -> 139 us (0.48); the launches traced: 282 us -> 137 us
  waiting for transfers between devices: 125 us -> 45 us
  local copies, waits for them, and re-layouts: 75.3 us -> 6.15 us
  blocking collectives: 5.67 us -> 39.1 us
  matrix products: 25.2 us -> 1.56 us
  Pallas kernels: 0 us -> 10.6 us
  starting transfers between devices: 26.5 us -> 19 us
  other arithmetic: 8.87 us -> 1.59 us
    all_gather x1, waiting for transfers between devices: 123 us -> 18.4 us  [gather_params(): mine = lax.all_gather(held, axes, axis_index_groups=along_y[0] + along_z[1])]
    all_gather x0 -> x1, blocking collectives: none -> 34.2 us  [gather_params(): held = lax.all_gather(pair, axes, axis_index_groups=along_z[0] + along_y[1])]
    ppermute x8 -> x5, waiting for transfers between devices: 1.98 us -> 26.7 us  [the longest x2 12.7 us: neighbours(): lax.ppermute(tail, axes, [(i, (i + 1) % count) for i in range(ends)])]
    reshape x12 -> x5, local copies, waits for them, and re-layouts: 23 us -> 1.91 us  [the longest x1 0.94 us: gather_params(): coarse = coarse_params.reshape(-1, 2 * channels)]
    dot_general x15 -> x2, matrix products: 20.1 us -> 1.56 us  [dot(): return jnp.dot(left, right, preferred_element_type=jnp.float32)]
    unnamed x27 -> x14, local copies, waits for them, and re-layouts: 20 us -> 3.03 us
    slice x8 -> x0, local copies, waits for them, and re-layouts: 15.3 us -> none  [the longest x1 11 us: gather_params(): return (every[:, :fine_rows].reshape(-1), every[:, fine_rows:].reshape(-1))]
    pallas_call x0 -> x1, Pallas kernels: none -> 10.6 us  [run(): pl.pallas_call(kernel, out_shape=(jax.ShapeDtypeStruct((ROWS * COLS, chan...]
  transfers between devices with their start and end apart: 9 -> 6, of which waited for: 2 -> 5; matrix products, arithmetic and copies ran while one was open for 16% -> 3% of each run, Pallas kernels for 0% -> 0%
where the time goes in v2:
time: 139 us; the launch traced here: 137 us
  waiting for transfers between devices  45 us (32%)
  blocking collectives  39.1 us (28%)
  starting transfers between devices  19 us (14%)
  between operations  14.4 us (10%)
  Pallas kernels  10.6 us (8%)
  local copies, waits for them, and re-layouts  6.15 us (4%)
  other arithmetic  1.59 us (1%)
  matrix products  1.56 us (1%)
    all_gather x1, blocking collectives, gather_params(): held = lax.all_gather(pair, axes, axis_index_groups=along_z[0] + along_y[1])  34.2 us
    all_gather x1, waiting for transfers between devices, gather_params(): mine = lax.all_gather(held, axes, axis_index_groups=along_y[0] + along_z[1])  18.4 us
    ppermute x2, waiting for transfers between devices, neighbours(): lax.ppermute(tail, axes, [(i, (i + 1) % count) for i in range(ends)])  12.7 us
    ppermute x1, waiting for transfers between devices, local(): other = lax.ppermute(mine, 'c', [(0, 1), (1, 0)])  11.2 us
    pallas_call x1, Pallas kernels, run(): pl.pallas_call(kernel, out_shape=(jax.ShapeDtypeStruct((ROWS * COLS, chan...  10.6 us
    ppermute x2, starting transfers between devices, neighbours(): lax.ppermute(head, axes, [((i + 1) % count, i) for i in range(ends)])  9.68 us
    ppermute x1, starting transfers between devices, local(): other = lax.ppermute(mine, 'c', [(0, 1), (1, 0)])  4.96 us
    all_gather x1, blocking collectives, gather_params(): pair = lax.all_gather(packed, 'xl', axis=0, tiled=False)  4.85 us
  transfers between devices with their start and end apart: 6, of which 5 were waited for; matrix products, arithmetic and copies ran while one was open for 3% of the time, Pallas kernels for 0%

profile of v2, /device:TPU:6, one launch (start us, length us, event | category | flops | bytes accessed | tf_op | source)
XLA Modules:
  0.0 137.4 jit_solution(12214005596017579627)
XLA Ops:
  7.2 0.0 copy-start.6
  7.2 0.0 copy-start.2
  7.2 0.0 copy-start.1
  7.2 0.0 all-gather.4.cloned.1.call-start
  7.2 0.8 reshape.164
  8.0 0.9 reshape.163
  9.0 4.9 %all_gather.16 = bf16[2,112,256]{2,1,0:T(8,128)(2,1)S(1)} all-gather(bf16[1,112,256]{2,1,0:T(8,128)(2,1)S(1)} %maximum_select_fusion), channel_id=1, replica_groups=mesh['xl'=2,'y'=8,'z'=8,'xh'=2,'c'=2] {'xl'}, dimensions={0}, use_global_device_ids=true | all-gather | bytes 172032 | tf_op jit(solution)/shard_map/all_gather | solution.py:378
  13.9 34.2 %all-gather = bf16[16,112,256]{2,1,0:T(8,128)(2,1)} all-gather(bf16[2,112,256]{2,1,0:T(8,128)(2,1)S(1)} %all_gather.16), channel_id=2, replica_groups={{0,4,8,12,16,20,24,28},{32,36,40,44,48,52,56,60},{64,68,72,76,80,84,88,..., dimensions={0}, use_global_device_ids=true | all-gather | bytes 1032192 | tf_op jit(solution)/shard_map/all_gather | solution.py:385
  48.1 0.0 all-gather.4.cloned.1.call-update
  48.1 0.0 copy-done.2
  48.2 0.1 broadcast_in_dim.42
  48.3 0.0 copy-done.1
  48.3 1.9 %collective-permute-start.1 = (bf16[3,24,640]{2,1,0:T(8,128)(2,1)S(1)}, bf16[3,24,640]{2,1,0:T(8,128)(2,1)S(1)}, u32[]{:S(2)}, u32[]{:S(2)}) collective-permute-start(bf16[3,24,640]{2,1,0:T(8,128)(2,1)S(1)} %get-tuple-element.18), channel_id=1, source_target_pairs={{1,0},{2,1},{3,2},{5,4},{6,5},{7,6},{9,8},{10,9},{11,10},{13,12},{... | collective-permute-start | bytes 276488 | tf_op jit(solution)/shard_map/ppermute | solution.py:358
  50.2 2.4 %collective-permute-start = (bf16[3,24,640]{2,1,0:T(8,128)(2,1)S(1)}, bf16[3,24,640]{2,1,0:T(8,128)(2,1)S(1)}, u32[]{:S(2)}, u32[]{:S(2)}) collective-permute-start(bf16[3,24,640]{2,1,0:T(8,128)(2,1)S(1)} %get-tuple-element.19), channel_id=1, source_target_pairs={{0,1},{1,2},{2,3},{4,5},{5,6},{6,7},{8,9},{9,10},{10,11},{12,13},{... | collective-permute-start | bytes 276488 | tf_op jit(solution)/shard_map/ppermute | solution.py:357
  52.7 0.1 reshape.169
  52.8 0.2 reduce_max.9
  53.0 0.1 gt.33
  53.0 0.0 copy-done.6
  53.0 0.4 convolution_convert_fusion.cells
  53.5 0.0 copy-start.5
  53.5 0.0 collective-permute-done.1
  53.5 4.1 %collective-permute-done = bf16[3,24,640]{2,1,0:T(8,128)(2,1)S(1)} collective-permute-done((bf16[3,24,640]{2,1,0:T(8,128)(2,1)S(1)}, bf16[3,24,640]{2,1,0:T(8,128)(2,1)S(1)}, u32[]{:S(2)}, u32[]{:S(2)}) %collective-permute-start) | collective-permute-done | bytes 92192 | tf_op jit(solution)/shard_map/ppermute | solution.py:357
  57.6 0.1 pad_maximum_fusion.1
  57.7 7.8 %collective-permute-start.3 = (bf16[18,6,640]{2,1,0:T(8,128)(2,1)S(1)}, bf16[18,6,640]{2,1,0:T(8,128)(2,1)S(1)}, u32[]{:S(2)}, u32[]{:S(2)}) collective-permute-start(bf16[18,6,640]{2,1,0:T(8,128)(2,1)S(1)} %get-tuple-element.16), channel_id=1, source_target_pairs={{4,0},{8,4},{12,8},{16,12},{20,16},{24,20},{28,24},{32,28},{36,32}... | collective-permute-start | bytes 414728 | tf_op jit(solution)/shard_map/ppermute | solution.py:358
  65.4 1.9 %collective-permute-start.2 = (bf16[18,6,640]{2,1,0:T(8,128)(2,1)S(1)}, bf16[18,6,640]{2,1,0:T(8,128)(2,1)S(1)}, u32[]{:S(2)}, u32[]{:S(2)}) collective-permute-start(bf16[18,6,640]{2,1,0:T(8,128)(2,1)S(1)} %get-tuple-element.17), channel_id=1, source_target_pairs={{0,4},{4,8},{8,12},{12,16},{16,20},{20,24},{24,28},{28,32},{32,36}... | collective-permute-start | bytes 414728 | tf_op jit(solution)/shard_map/ppermute | solution.py:357
  67.4 0.1 broadcast_in_dim.40
  67.5 0.1 broadcast_in_dim.41
  67.6 2.8 %collective-permute-done.3 = bf16[18,6,640]{2,1,0:T(8,128)(2,1)S(1)} collective-permute-done((bf16[18,6,640]{2,1,0:T(8,128)(2,1)S(1)}, bf16[18,6,640]{2,1,0:T(8,128)(2,1)S(1)}, u32[]{:S(2)}, u32[]{:S(2)}) %collective-permute-start.3) | collective-permute-done | bytes 138272 | tf_op jit(solution)/shard_map/ppermute | solution.py:358
  70.4 0.1 reshape.168
  70.5 8.6 %collective-permute-done.2 = bf16[18,6,640]{2,1,0:T(8,128)(2,1)S(1)} collective-permute-done((bf16[18,6,640]{2,1,0:T(8,128)(2,1)S(1)}, bf16[18,6,640]{2,1,0:T(8,128)(2,1)S(1)}, u32[]{:S(2)}, u32[]{:S(2)}) %collective-permute-start.2) | collective-permute-done | bytes 138272 | tf_op jit(solution)/shard_map/ppermute | solution.py:357
  79.1 0.1 reshape.167
  79.1 0.7 concatenate.58
  79.8 0.0 copy-done.5
  79.9 1.1 fusion
  81.0 0.2 fusion.4
  81.2 0.1 gt.30
  81.3 0.2 slice_reduce_fusion
  81.5 0.0 copy-start.4
  81.5 0.0 copy-start.3
  81.5 0.3 multiply_reduce_fusion
  81.9 0.3 multiply_convert_fusion.tokens
  82.2 18.4 %all-gather.4.cloned.1.call-done = bf16[64,2,112,256]{3,2,1,0:T(8,128)(2,1)} async-done(((bf16[8,2,112,256]{3,2,1,0:T(8,128)(2,1)}), bf16[64,2,112,256]{3,2,1,0:T(8,128)(2,1)}) %all-gather.4.cloned.1.call-update) | async-done | bytes 7340048 | tf_op jit(solution)/shard_map/all_gather | solution.py:386
  100.5 5.0 %collective-permute-start.4 = (bf16[8,8,2,112,256]{4,3,2,1,0:T(8,128)(2,1)}, bf16[8,8,2,112,256]{4,3,2,1,0:T(8,128)(2,1)S(1)}, u32[]{:S(2)}, u32[]{:S(2)}) collective-permute-start(bf16[8,8,2,112,256]{4,3,2,1,0:T(8,128)(2,1)} %bitcast.23), channel_id=1, source_target_pairs={{0,1},{1,0},{2,3},{3,2},{4,5},{5,4},{6,7},{7,6},{8,9},{9,8},{10,11... | collective-permute-start | bytes 22020104 | tf_op jit(solution)/shard_map/ppermute | solution.py:418
  105.5 0.0 copy-done.4
  105.5 0.1 fusion.3.back
  105.6 0.0 copy-done.3
  105.6 0.1 fusion.2.from_blended
  105.8 11.2 %collective-permute-done.4.other = bf16[8,8,2,112,256]{4,3,2,1,0:T(8,128)(2,1)S(1)} collective-permute-done((bf16[8,8,2,112,256]{4,3,2,1,0:T(8,128)(2,1)}, bf16[8,8,2,112,256]{4,3,2,1,0:T(8,128)(2,1)S(1)}, u32[]{:S(2)}, u32[]{:S(2)}) %collective-permute-start.4) | collective-permute-done | bytes 7340064 | tf_op jit(solution)/shard_map/ppermute | solution.py:418
  117.0 0.0 copy-start
  117.0 3.0 %copy-done = bf16[8,8,2,112,256]{4,3,2,1,0:T(8,128)(2,1)} copy-done((bf16[8,8,2,112,256]{4,3,2,1,0:T(8,128)(2,1)}, bf16[8,8,2,112,256]{4,3,2,1,0:T(8,128)(2,1)S(1)}, u32[]{:S(2)}) %copy-start) | copy-done | bytes 7340056
  120.0 10.6 %shard_map.95 = (bf16[288,512]{1,0:T(8,128)(2,1)}, bf16[6,12,1024]{2,1,0:T(8,128)(2,1)}) custom-call(s32[1]{0:T(128)} %bitcast.core, bf16[720,512]{1,0:T(8,128)(2,1)S(1)} %multiply_convert_fusion.tokens, f32[9,80,80]{2,1,0:T(8,128)S(1)} %or_select_fusion.bias, bf16[384,512]{1,0:T(8,128)(2,1)S(1)} %convolution_convert_fusion.cells, ...), custom_call_target="tpu_custom_call" | custom-call | flops 4000000000 | bytes 18000000 | tf_op jit(solution)/shard_map/pallas_call | solution.py:314
  (12 shorter events, 0.2 us)
Async XLA Ops:
  7.2 45.9 %copy-start.6 = (s32[384]{0:T(512)S(1)}, s32[384]{0:T(512)}, u32[]{:S(2)}) copy-start(s32[384]{0:T(512)} %constant.29.clone) | copy-start | bytes 4612
  7.2 41.0 %copy-start.2 = (s32[12,24]{1,0:T(8,128)S(1)}, s32[12,24]{1,0:T(8,128)}, u32[]{:S(2)}) copy-start(s32[12,24]{1,0:T(8,128)} %param.9) | copy-start | bytes 3460
  7.2 41.1 %copy-start.1 = (bf16[1,12,24,512]{3,2,1,0:T(8,128)(2,1)S(1)}, bf16[1,12,24,512]{3,2,1,0:T(8,128)(2,1)}, u32[]{:S(2)}) copy-start(bf16[1,12,24,512]{3,2,1,0:T(8,128)(2,1)} %param.8) | copy-start | bytes 884740
  7.2 93.3 %all-gather.4.cloned.1.call-start = ((), (), s32[]{:S(2)}) async-start(), calls=%async_computation | async-start | bytes 8257536 | tf_op jit(solution)/shard_map/all_gather | solution.py:386
  48.3 5.2 %collective-permute-start.1 = (bf16[3,24,640]{2,1,0:T(8,128)(2,1)S(1)}, bf16[3,24,640]{2,1,0:T(8,128)(2,1)S(1)}, u32[]{:S(2)}, u32[]{:S(2)}) collective-permute-start(bf16[3,24,640]{2,1,0:T(8,128)(2,1)S(1)} %get-tuple-element.18), channel_id=1, source_target_pairs={{1,0},{2,1},{3,2},{5,4},{6,5},{7,6},{9,8},{10,9},{11,10},{13,12},{... | collective-permute-start | bytes 276488 | tf_op jit(solution)/shard_map/ppermute | solution.py:358
  50.2 7.4 %collective-permute-start = (bf16[3,24,640]{2,1,0:T(8,128)(2,1)S(1)}, bf16[3,24,640]{2,1,0:T(8,128)(2,1)S(1)}, u32[]{:S(2)}, u32[]{:S(2)}) collective-permute-start(bf16[3,24,640]{2,1,0:T(8,128)(2,1)S(1)} %get-tuple-element.19), channel_id=1, source_target_pairs={{0,1},{1,2},{2,3},{4,5},{5,6},{6,7},{8,9},{9,10},{10,11},{12,13},{... | collective-permute-start | bytes 276488 | tf_op jit(solution)/shard_map/ppermute | solution.py:357
  53.5 26.4 %copy-start.5 = (s32[720]{0:T(1024)S(1)}, s32[720]{0:T(1024)}, u32[]{:S(2)}) copy-start(s32[720]{0:T(1024)} %constant.28.clone) | copy-start | bytes 8644
  57.7 12.8 %collective-permute-start.3 = (bf16[18,6,640]{2,1,0:T(8,128)(2,1)S(1)}, bf16[18,6,640]{2,1,0:T(8,128)(2,1)S(1)}, u32[]{:S(2)}, u32[]{:S(2)}) collective-permute-start(bf16[18,6,640]{2,1,0:T(8,128)(2,1)S(1)} %get-tuple-element.16), channel_id=1, source_target_pairs={{4,0},{8,4},{12,8},{16,12},{20,16},{24,20},{28,24},{32,28},{36,32}... | collective-permute-start | bytes 414728 | tf_op jit(solution)/shard_map/ppermute | solution.py:358
  65.4 13.6 %collective-permute-start.2 = (bf16[18,6,640]{2,1,0:T(8,128)(2,1)S(1)}, bf16[18,6,640]{2,1,0:T(8,128)(2,1)S(1)}, u32[]{:S(2)}, u32[]{:S(2)}) collective-permute-start(bf16[18,6,640]{2,1,0:T(8,128)(2,1)S(1)} %get-tuple-element.17), channel_id=1, source_target_pairs={{0,4},{4,8},{8,12},{12,16},{16,20},{20,24},{24,28},{28,32},{32,36}... | collective-permute-start | bytes 414728 | tf_op jit(solution)/shard_map/ppermute | solution.py:357
  81.5 24.0 %copy-start.4 = (s32[288]{0:T(512)S(1)}, s32[288]{0:T(512)}, u32[]{:S(2)}) copy-start(s32[288]{0:T(512)} %constant.31.clone) | copy-start | bytes 3460
  81.5 24.1 %copy-start.3 = (s32[384]{0:T(512)S(1)}, s32[384]{0:T(512)}, u32[]{:S(2)}) copy-start(s32[384]{0:T(512)} %constant.30.clone) | copy-start | bytes 4612
  100.5 16.4 %collective-permute-start.4 = (bf16[8,8,2,112,256]{4,3,2,1,0:T(8,128)(2,1)}, bf16[8,8,2,112,256]{4,3,2,1,0:T(8,128)(2,1)S(1)}, u32[]{:S(2)}, u32[]{:S(2)}) collective-permute-start(bf16[8,8,2,112,256]{4,3,2,1,0:T(8,128)(2,1)} %bitcast.23), channel_id=1, source_target_pairs={{0,1},{1,0},{2,3},{3,2},{4,5},{5,4},{6,7},{7,6},{8,9},{9,8},{10,11... | collective-permute-start | bytes 22020104 | tf_op jit(solution)/shard_map/ppermute | solution.py:418
  117.0 3.0 %copy-start = (bf16[8,8,2,112,256]{4,3,2,1,0:T(8,128)(2,1)}, bf16[8,8,2,112,256]{4,3,2,1,0:T(8,128)(2,1)S(1)}, u32[]{:S(2)}) copy-start(bf16[8,8,2,112,256]{4,3,2,1,0:T(8,128)(2,1)S(1)} %collective-permute-done.4.other) | copy-start | bytes 22020100
Sparse Core Ops, SparseCore 0:
  48.3 52.2 all-gather.3
